TPU v7x, 256 devices: a whole 4x4x8 slice. The times are simulated.
256 devices in a mesh: row: 8 (over z_lo, x), col: 32 (over y, z_hi, core).
Axes of the slice: x: 4, y: 4, z: 8 (z_hi: 4, z_lo: 2; z = z_hi * 2 + z_lo), core: 2. Of those that a mesh axis runs over, the one named last changes fastest.
Arguments:
- adj_trailing: float32 [8192, 8192], P('row', 'col'), may hold values from -6 to 6
- panel: float32 [8192, 512], P('row', 'col'), may hold values from -0.0625 to 0.0625
- panel_adjoint: float32 [8192, 512], P('row', 'col'), may hold values from -6 to 6
- inverse_diag: float32 [512, 512], replicated, as said below
Outputs:
- grad_block: float32 [8192, 512], P('row', 'col')
- diag_grad: float32 [512, 512], P('col')
Inputs may be any that keep to these rules, and one draw needn't show every extreme that they name: `inverse_diag`: lower triangular, with a diagonal of 0.5 to 1.5.
All inputs are finite; a program needn't handle non-finite values.
Results may differ from a plain program's by a relative error of at most 0.000088.
Values sent between devices are 32-bit elements; how exact they have to be, the bound alone decides.
A program may use at most 64 MiB of HBM per device.

v0:
```python
import functools

import jax
import jax.numpy as jnp
from jax import lax
from jax.experimental import pallas as pl
from jax.experimental.pallas import tpu as pltpu
from jax.sharding import PartitionSpec as P

F32 = jnp.float32
BF16 = jnp.bfloat16
MESH = pl.DeviceIdType.MESH
NT = (((1,), (1,)), ((), ()))


def split(value):
    high = value.astype(BF16)
    low = (value - high.astype(F32)).astype(BF16)
    return high, low


def dot3(a_high, a_low, b_high, b_low):
    def one(a, b):
        return lax.dot_general(a, b, NT, preferred_element_type=F32)

    return one(a_high, b_low) + one(a_low, b_high) + one(a_high, b_high)


def aligned(start, size):
    return pl.ds(pl.multiple_of(start, size), size)


def kernel(
    a_hbm, panel_hbm, pa_hbm, inv_hbm, grad_ref, diag_ref,
    panel_v, pa_v, inv_v, wide, s_raw, pf, pc, s_hi, s_lo, st_hi, st_lo,
    p_hi, p_lo, f_hi, f_lo, inv_r, it_hi, it_lo, iq_hi, iq_lo, pa_r, out1, out2, ry, rr,
    qadj, gq, rgq, adj, gt, rg, gfull, dpart, rd,
    local_sem, agz_s, agz_r, agy_s, agy_r, sa_s, sa_r, mini_s, mini_r, pc_s, pc_r, po_s, po_r,
    ry_s, ry_r, rr_s, rr_r, f_s, f_r, rgq_s, rgq_r, rg_s, rg_r, rd_s, rd_r,
):
    r = lax.axis_index("row")
    c = lax.axis_index("col")
    zl, x = r // 4, r % 4
    y, z, p = c // 8, (c // 2) % 4, c % 2
    yz = y * 4 + z

    def dev(zl_, x_, y_, z_, p_):
        return (zl_ * 4 + x_, (y_ * 4 + z_) * 2 + p_)

    def remote(src, dst, send, recv, target):
        return pltpu.make_async_remote_copy(
            src_ref=src, dst_ref=dst, send_sem=send, recv_sem=recv,
            device_id=target, device_id_type=MESH,
        )

    sibling = dev(zl, x, y, z, 1 - p)

    def arrived(ref, send, recv):
        remote(ref, ref, send, recv, sibling).wait_recv()

    barrier = pltpu.get_barrier_semaphore()
    greet = [sibling]
    greet += [dev(zl, x, y, (z + j) % 4, p) for j in (1, 2, 3)]
    greet += [dev(zl, x, (y + j) % 4, z, p) for j in (1, 2, 3)]
    row_offsets = [(a, b) for a in (0, 1) for b in (0, 1, 2, 3) if (a, b) != (0, 0)]
    greet += [dev((zl + a) % 2, (x + b) % 4, y, z, p) for a, b in row_offsets]
    for target in greet:
        pl.semaphore_signal(barrier, inc=1, device_id=target, device_id_type=MESH)
    to_row, to_z = (z // 2) * 4 + y, r // 2
    keeps = jnp.logical_and(to_row == r, to_z == z)
    for b in (0, 1):
        for h in (0, 1):
            is_me = jnp.logical_and(keeps, jnp.logical_and(r % 2 == b, z % 2 == h))

            @pl.when(jnp.logical_not(is_me))
            def _():
                pl.semaphore_signal(
                    barrier, inc=1, device_id=(2 * z + b, (x * 4 + zl * 2 + h) * 2 + p),
                    device_id_type=MESH,
                )

    load_panel = pltpu.make_async_copy(panel_hbm, panel_v, local_sem.at[0])
    load_a = pltpu.make_async_copy(a_hbm, s_raw.at[p], local_sem.at[1])
    load_pa = pltpu.make_async_copy(pa_hbm, pa_v, local_sem.at[2])
    load_inv = pltpu.make_async_copy(inv_hbm, inv_v, local_sem.at[3])
    load_panel.start()
    load_a.start()
    load_pa.start()
    load_inv.start()

    left = lax.broadcasted_iota(jnp.int32, (16, 128), 1) < 64

    def ordered(ref, t):
        w1 = t // 2 + 8 * (t % 2)
        one = ref[:, 128 * (w1 // 2):128 * (w1 // 2) + 128]
        two = ref[:, 128 * (w1 // 2 + 2):128 * (w1 // 2 + 2) + 128]
        if w1 % 2:
            one = pltpu.roll(one, 64, 1)
        else:
            two = pltpu.roll(two, 64, 1)
        return jnp.where(left, one, two)

    load_panel.wait()
    for t in range(8):
        pf[yz, p, :, 128 * t:128 * t + 128] = ordered(panel_v, t)

    pl.semaphore_wait(barrier, len(greet) + 3 + jnp.where(keeps, 0, 1))

    sends = []
    conditional = []

    def drain():
        while sends:
            sends.pop().wait_send()
        while conditional:
            cond, cp = conditional.pop()
            pl.when(cond)(cp.wait_send)


    for j in (2, 1, 3, 0):
        y2 = (y + j) % 4
        src = pf.at[yz, p, :, aligned(256 * y2, 256)]
        dst = pc.at[aligned(16 * yz, 16), aligned(256 * (r % 2), 256)]
        cp = remote(src, dst, mini_s.at[j], mini_r.at[r % 2, z % 2], (to_row, (y2 * 4 + to_z) * 2 + p))
        if j:
            cp.start()
            sends.append(cp)
        else:
            pl.when(jnp.logical_not(keeps))(cp.start)
            conditional.append((jnp.logical_not(keeps), cp))

    @pl.when(keeps)
    def _():
        pc[aligned(16 * yz, 16), aligned(256 * (r % 2), 256)] = pf[yz, p, :, aligned(256 * y, 256)]

    for j in (1, 3, 2):
        cp = remote(pf.at[yz, p], pf.at[yz, p], agz_s.at[j], agz_r.at[j], dev(zl, x, y, (z + j) % 4, p))
        cp.start()
        sends.append(cp)

    def forward_y(k):
        slot = y * 4 + (z + 4 - k) % 4
        for j in (1, 3, 2):
            cp = remote(
                pf.at[slot, p], pf.at[slot, p], agy_s.at[j, k], agy_r.at[j, k],
                dev(zl, x, (y + j) % 4, z, p),
            )
            cp.start()
            sends.append(cp)

    forward_y(0)
    load_a.wait()
    cp_a = remote(s_raw.at[p], s_raw.at[p], sa_s, sa_r, sibling)
    cp_a.start()
    sends.append(cp_a)

    lane = lax.broadcasted_iota(jnp.int32, (128, 256), 1)
    line = lax.broadcasted_iota(jnp.int32, (128, 256), 0)

    def col_nat(b):
        return (32 * (lane // 64) + c - p + b) * 64 + lane % 64

    def prepare(b):
        cols = (32 * (lane // 64) + c - p + b) * 64 + lane % 64

        def step(t, carry):
            w1 = t // 2 + 8 * (t % 2)
            rows = jnp.concatenate(
                [s_raw[b, aligned(64 * w1, 64), :], s_raw[b, aligned(64 * w1 + 256, 64), :]], axis=0
            )
            row_nat = (8 * w1 + r) * 64 + line + jnp.where(line >= 64, 32 * 64 - 64, 0)
            value = jnp.where(row_nat >= cols, rows, 0.0)
            high, low = split(value)
            s_hi[aligned(128 * t, 128), aligned(256 * b, 256)] = high
            s_lo[aligned(128 * t, 128), aligned(256 * b, 256)] = low
            high, low = split(value.T)
            st_hi[aligned(256 * b, 256), aligned(128 * t, 128)] = high
            st_lo[aligned(256 * b, 256), aligned(128 * t, 128)] = low
            return carry

        lax.fori_loop(0, 8, step, 0)

    for k in (1, 3, 2):
        arrived(pf.at[0, 0], agz_s.at[k], agz_r.at[k])
        forward_y(k)

    for b in (0, 1):
        for h in (0, 1):
            is_me = jnp.logical_and(keeps, jnp.logical_and(r % 2 == b, z % 2 == h))

            @pl.when(jnp.logical_not(is_me))
            def _():
                arrived(pc.at[0:16, 0:256], mini_s.at[0], mini_r.at[b, h])

    part = pc.at[aligned(32 * (2 * x + zl), 32)]
    for a, b in ((1, 2), (1, 1), (1, 3), (1, 0), (0, 2), (0, 1), (0, 3)):
        cp = remote(part, part, pc_s.at[a, b], pc_r.at[a, b], dev((zl + a) % 2, (x + b) % 4, y, z, p))
        cp.start()
        sends.append(cp)
    prepare(p)
    load_pa.wait()
    wide[...] = jnp.zeros_like(wide)
    for t in range(8):
        wide[aligned(16 * (yz % 8), 16), 128 * t:128 * t + 128] = ordered(pa_v, t)
    for t in range(8):
        pa_r[128 * t:128 * t + 128, :] = wide[:, 128 * t:128 * t + 128].T

    arrived(s_raw.at[0], sa_s, sa_r)
    prepare(1 - p)
    for a, b in row_offsets:
        arrived(pc.at[0:32], pc_s.at[a, b], pc_r.at[a, b])

    pc_hi, pc_lo = split(pc[...])
    tile = aligned(128 * (y // 2), 128)
    for h, j in ((0, 1), (0, 3), (0, 2), (1, 1), (1, 3), (1, 2)):
        rows = aligned(256 * ((y + j) % 4) + 128 * h, 128)
        out1[rows, :] = dot3(s_hi[rows, :], s_lo[rows, :], pc_hi, pc_lo)
        out1[rows, tile] = out1[rows, tile] - pa_r[rows, :]
        cp = remote(
            out1.at[rows], ry.at[j, h], ry_s.at[j, h], ry_r.at[j, h], dev(zl, x, (y + j) % 4, z, p)
        )
        cp.start()
        sends.append(cp)

    for j in (1, 3, 2):
        for k in range(4):
            arrived(pf.at[0, 0], agy_s.at[j, k], agy_r.at[j, k])
    cp = remote(pf.at[:, p], pf.at[:, p], po_s, po_r, sibling)
    cp.start()
    sends.append(cp)
    for k in range(16):
        high, low = split(pf[k, p])
        p_hi[16 * k:16 * k + 16, :] = high
        p_lo[16 * k:16 * k + 16, :] = low
    for b in (0, 1):
        rows = pl.ds(256 * b, 256)
        out2[rows, :] = dot3(st_hi[rows, :], st_lo[rows, :], p_hi[...], p_lo[...])
    for i, (a, b) in enumerate(row_offsets):
        piece = ((zl + a) % 2) * 4 + (x + b) % 4
        cp = remote(
            out2.at[aligned(64 * piece, 64)], rr.at[i], rr_s.at[i], rr_r.at[i],
            dev((zl + a) % 2, (x + b) % 4, y, z, p),
        )
        cp.start()
        sends.append(cp)

    for h in (0, 1):
        rows = aligned(256 * y + 128 * h, 128)
        out1[rows, :] = dot3(s_hi[rows, :], s_lo[rows, :], pc_hi, pc_lo)
        out1[rows, tile] = out1[rows, tile] - pa_r[rows, :]

    load_inv.wait()
    for k in range(16):
        for b in (0, 1):
            inv_r[256 * b + 16 * k:256 * b + 16 * k + 16, :] = -inv_v[(2 * k + b) * 16:(2 * k + b) * 16 + 16, :]
    for t in range(4):
        inv_v[128 * t:128 * t + 128, :] = inv_r[:, 128 * t:128 * t + 128].T
    for k in range(16):
        high, low = split(inv_v[aligned((2 * k + p) * 16, 16), :])
        it_hi[16 * k:16 * k + 16, :] = high
        it_lo[16 * k:16 * k + 16, :] = low

    for k in range(8):
        for e in (0, 1):
            first = inv_v[aligned((4 * k + p) * 16 + 8 * e, 8), :]
            second = inv_v[aligned((4 * k + 2 + p) * 16 + 8 * e, 8), :]
            high, low = split(jnp.concatenate([first, second], axis=0))
            iq_hi[e, 16 * k:16 * k + 16, :] = high
            iq_lo[e, 16 * k:16 * k + 16, :] = low

    own = aligned(256 * p, 256)
    offsets = [(dy, dz) for dz in (2, 1, 3, 0) for dy in (2, 1, 3, 0)]
    others = offsets[:-1]

    def swap(ref, k):
        cp = remote(ref, ref, f_s.at[k], f_r.at[k], sibling)
        cp.start()
        sends.append(cp)

    def sum_y(h):
        for j in (1, 3, 2):
            arrived(ry.at[0, 0], ry_s.at[j, h], ry_r.at[j, h])
        adj[h, :, own] = (
            out1[aligned(256 * y + 128 * h, 128), :] + ry[1, h] + ry[2, h] + ry[3, h]
        )
        swap(adj.at[h, :, own], h)

    def to_owners(h):
        arrived(adj.at[h, :, 0:256], f_s.at[h], f_r.at[h])
        a_hi, a_lo = split(adj[h])
        gt[h] = dot3(it_hi[...], it_lo[...], a_hi, a_lo)
        for dy, dz in others:
            i = dy * 4 + dz
            y2, z2 = (y + dy) % 4, (z + dz) % 4
            cp = remote(
                gt.at[h, aligned(16 * (y2 * 4 + z2), 16)], rg.at[h, yz], rg_s.at[h, i], rg_r.at[h, i],
                dev(zl, x, y2, z2, p),
            )
            cp.start()
            sends.append(cp)
        rg[h, yz] = gt[h, aligned(16 * yz, 16), :]

    sum_y(0)
    to_owners(0)

    total = out2[aligned(64 * r, 64), :]
    for i in range(7):
        arrived(rr.at[i], rr_s.at[i], rr_r.at[i])
        total = total + rr[i]
    qadj[:, own] = total
    swap(qadj.at[:, own], 2)
    sum_y(1)

    arrived(qadj.at[:, 0:256], f_s.at[2], f_r.at[2])
    a_hi, a_lo = split(qadj[...])
    none = jnp.zeros((64, 512), BF16)
    gq[...] = dot3(
        iq_hi[0], iq_lo[0], jnp.concatenate([a_hi, none], axis=0), jnp.concatenate([a_lo, none], axis=0)
    ) + dot3(
        iq_hi[1], iq_lo[1], jnp.concatenate([none, a_hi], axis=0), jnp.concatenate([none, a_lo], axis=0)
    )
    q_row, q_slot = 2 * z + zl, y * 4 + x
    stays = q_row == r
    moves = jnp.logical_not(stays)
    for dy, dz in offsets:
        i = dy * 4 + dz
        to = ((y + dy) % 4) * 4 + (z + dz) % 4
        cp = remote(
            gq.at[aligned(8 * to, 8)], rgq.at[q_slot], rgq_s.at[i], rgq_r.at[q_slot], (q_row, to * 2 + p)
        )
        if i:
            cp.start()
            sends.append(cp)
        else:
            pl.when(moves)(cp.start)
            conditional.append((moves, cp))

    @pl.when(stays)
    def _():
        rgq[q_slot] = gq[aligned(8 * yz, 8), :]

    to_owners(1)

    arrived(pf.at[:, 0], po_s, po_r)
    for k in range(16):
        for b in (0, 1):
            high, low = split(pf[k, b])
            f_hi[32 * k + 16 * b:32 * k + 16 * b + 16, :] = high
            f_lo[32 * k + 16 * b:32 * k + 16 * b + 16, :] = low

    drain()
    for h in (0, 1):
        for dy, dz in others:
            i = dy * 4 + dz
            arrived(rg.at[0, 0], rg_s.at[h, i], rg_r.at[h, i])
    for slot in range(16):
        @pl.when(jnp.logical_not(jnp.logical_and(stays, q_slot == slot)))
        def _():
            arrived(rgq.at[0], rgq_s.at[0], rgq_r.at[slot])

    low_half = left[0:8]
    for t in range(8):
        h, g = t % 2, 4 * (t // 2)
        parts = (rg[h, g] + rg[h, g + 1]) + (rg[h, g + 2] + rg[h, g + 3])
        one, two = rgq[2 * t], rgq[2 * t + 1]
        upper = jnp.where(low_half, one, pltpu.roll(two, 64, 1))
        lower = jnp.where(low_half, pltpu.roll(one, 64, 1), two)
        gfull[:, 128 * t:128 * t + 128] = parts + jnp.concatenate([upper, lower], axis=0)

    g_hi, g_lo = split(gfull[...])
    both = lax.dot_general(
        jnp.concatenate([g_hi, g_lo], axis=0), f_hi[...], NT, preferred_element_type=F32
    )
    cross = lax.dot_general(g_hi, f_lo[...], NT, preferred_element_type=F32)
    dpart[...] = both[0:16, :] + (both[16:32, :] + cross)
    for a, b in ((1, 2), (0, 2), (1, 1), (1, 3), (1, 0), (0, 1), (0, 3)):
        i = a * 4 + b - 1
        cp = remote(
            dpart, rd.at[i], rd_s.at[i], rd_r.at[i], dev((zl + a) % 2, (x + b) % 4, y, z, p)
        )
        cp.start()
        sends.append(cp)
    for t in range(8):
        w = 2 * t
        k1 = (w % 4) * 4 + w // 4
        k2 = k1 + 4
        one = gfull[:, 128 * (k1 // 2):128 * (k1 // 2) + 128]
        two = gfull[:, 128 * (k2 // 2):128 * (k2 // 2) + 128]
        if k1 % 2:
            one = pltpu.roll(one, 64, 1)
        else:
            two = pltpu.roll(two, 64, 1)
        grad_ref[:, 128 * t:128 * t + 128] = jnp.where(left, one, two)
    for i in range(7):
        arrived(rd.at[i], rd_s.at[i], rd_r.at[i])
    total = jnp.zeros((16, 512), F32)
    for q in range(8):
        a, b = (zl + 2 - q // 4) % 2, (x + 4 - q % 4) % 4
        slot = a * 4 + b
        keep = jnp.where(slot == 0, dpart[...], rd[jnp.maximum(slot - 1, 0)])
        total = total + keep
    diag_row = c * 16 + lax.broadcasted_iota(jnp.int32, (16, 512), 0)
    diag_col = lax.broadcasted_iota(jnp.int32, (16, 512), 1)
    diag_ref[...] = jnp.where(diag_row >= diag_col, -total, 0.0)

    drain()


def body(adj_trailing, panel, panel_adjoint, inverse_diag):
    vmem, dma = pltpu.VMEM, pltpu.SemaphoreType.DMA
    operands = (adj_trailing, panel.T, panel_adjoint.T, inverse_diag)
    grad, diag = pl.pallas_call(
        kernel,
        out_shape=(
            jax.ShapeDtypeStruct((16, 1024), F32),
            jax.ShapeDtypeStruct((16, 512), F32),
        ),
        in_specs=[pl.BlockSpec(memory_space=pl.ANY)] * 4,
        out_specs=(pl.BlockSpec(memory_space=vmem), pl.BlockSpec(memory_space=vmem)),
        scratch_shapes=[
            vmem((16, 1024), F32), vmem((16, 1024), F32), vmem((512, 512), F32), vmem((128, 1024), F32),
            vmem((2, 1024, 256), F32), vmem((16, 2, 16, 1024), F32), vmem((256, 512), F32),
            vmem((1024, 512), BF16), vmem((1024, 512), BF16), vmem((512, 1024), BF16), vmem((512, 1024), BF16),
            vmem((256, 1024), BF16), vmem((256, 1024), BF16), vmem((512, 1024), BF16), vmem((512, 1024), BF16),
            vmem((512, 512), F32), vmem((256, 512), BF16), vmem((256, 512), BF16),
            vmem((2, 128, 512), BF16), vmem((2, 128, 512), BF16), vmem((1024, 128), F32),
            vmem((1024, 256), F32), vmem((512, 256), F32), vmem((4, 2, 128, 256), F32), vmem((7, 64, 256), F32),
            vmem((64, 512), F32), vmem((128, 128), F32), vmem((16, 8, 128), F32),
            vmem((2, 128, 512), F32), vmem((2, 256, 128), F32), vmem((2, 16, 16, 128), F32), vmem((16, 1024), F32),
            vmem((16, 512), F32), vmem((7, 16, 512), F32),
            dma((4,)), dma((4,)), dma((4,)), dma((4, 4)), dma((4, 4)), dma, dma, dma((4,)), dma((2, 2)),
            dma((2, 4)), dma((2, 4)), dma, dma,
            dma((4, 2)), dma((4, 2)), dma((7,)), dma((7,)), dma((3,)), dma((3,)), dma((16,)), dma((16,)),
            dma((2, 16)), dma((2, 16)), dma((7,)), dma((7,)),
        ],
        compiler_params=pltpu.CompilerParams(
            collective_id=0, has_side_effects=True, vmem_limit_bytes=40 * 1024 * 1024
        ),
        name="cholesky_step",
    )(*(pltpu.with_memory_space_constraint(a, pltpu.HBM) for a in operands))
    return (grad.T, diag)


def solution(mesh):
    in_specs = (P("row", "col"), P("row", "col"), P("row", "col"), P())
    out_specs = (P("row", "col"), P("col", None))
    return jax.shard_map(body, mesh=mesh, in_specs=in_specs, out_specs=out_specs, check_vma=False)
```

profile of v0, /device:TPU:1, one launch (start us, length us, event | category | flops | bytes accessed | tf_op | source)
XLA Modules:
  0.0 61.4 jit_solution(17387342931372689165)
XLA Ops:
  0.6 59.5 %cholesky_step.1 = (f32[16,1024]{1,0:T(8,128)S(1)}, f32[16,512]{1,0:T(8,128)S(1)}) custom-call(f32[1024,256]{1,0:T(8,128)} %a_hbm.1, f32[16,1024]{1,0:T(8,128)} %bitcast.4, f32[16,1024]{1,0:T(8,128)} %bitcast.5, f32[512,512]{1,0:T(8,128)} %inv_hbm.1), custom_call_target="tpu_custom_call" | custom-call | tf_op jit(solution)/shard_map/cholesky_step/pallas_call | solution.py:412
  60.2 0.6 %copy.8 = f32[1024,16]{0,1:T(8,128)} copy(f32[1024,16]{0,1:T(8,128)S(1)} %bitcast.3) | data formatting | bytes 131072
  60.8 0.6 copy.9
where the time goes:
time: 61.5 us; the launch traced here: 61.4 us
  Pallas kernels  59.5 us (97%)
  local copies, waits for them, and re-layouts  1.25 us (2%)
  between operations  0.64 us (1%)
    pallas_call x1, Pallas kernels, body(): pl.pallas_call(kernel, out_shape=(jax.ShapeDtypeStruct((16, 1024), F32),...  59.5 us
    unnamed x2, local copies, waits for them, and re-layouts  1.25 us

commit v1 on v0

--- a/solution.py
+++ b/solution.py
@@ -265,8 +265,8 @@
             first = inv_v[aligned((4 * k + p) * 16 + 8 * e, 8), :]
             second = inv_v[aligned((4 * k + 2 + p) * 16 + 8 * e, 8), :]
             high, low = split(jnp.concatenate([first, second], axis=0))
-            iq_hi[e, 16 * k:16 * k + 16, :] = high
-            iq_lo[e, 16 * k:16 * k + 16, :] = low
+            iq_hi[128 * e + 16 * k:128 * e + 16 * k + 16, :] = high
+            iq_lo[128 * e + 16 * k:128 * e + 16 * k + 16, :] = low
 
     own = aligned(256 * p, 256)
     offsets = [(dy, dz) for dz in (2, 1, 3, 0) for dy in (2, 1, 3, 0)]
@@ -313,12 +313,8 @@
 
     arrived(qadj.at[:, 0:256], f_s.at[2], f_r.at[2])
     a_hi, a_lo = split(qadj[...])
-    none = jnp.zeros((64, 512), BF16)
-    gq[...] = dot3(
-        iq_hi[0], iq_lo[0], jnp.concatenate([a_hi, none], axis=0), jnp.concatenate([a_lo, none], axis=0)
-    ) + dot3(
-        iq_hi[1], iq_lo[1], jnp.concatenate([none, a_hi], axis=0), jnp.concatenate([none, a_lo], axis=0)
-    )
+    both = dot3(iq_hi[...], iq_lo[...], a_hi, a_lo)
+    gq[...] = jnp.concatenate([both[0:128, :], both[128:256, :]], axis=1)
     q_row, q_slot = 2 * z + zl, y * 4 + x
     stays = q_row == r
     moves = jnp.logical_not(stays)
@@ -423,7 +419,7 @@
             vmem((1024, 512), BF16), vmem((1024, 512), BF16), vmem((512, 1024), BF16), vmem((512, 1024), BF16),
             vmem((256, 1024), BF16), vmem((256, 1024), BF16), vmem((512, 1024), BF16), vmem((512, 1024), BF16),
             vmem((512, 512), F32), vmem((256, 512), BF16), vmem((256, 512), BF16),
-            vmem((2, 128, 512), BF16), vmem((2, 128, 512), BF16), vmem((1024, 128), F32),
+            vmem((256, 512), BF16), vmem((256, 512), BF16), vmem((1024, 128), F32),
             vmem((1024, 256), F32), vmem((512, 256), F32), vmem((4, 2, 128, 256), F32), vmem((7, 64, 256), F32),
             vmem((64, 512), F32), vmem((128, 128), F32), vmem((16, 8, 128), F32),
             vmem((2, 128, 512), F32), vmem((2, 256, 128), F32), vmem((2, 16, 16, 128), F32), vmem((16, 1024), F32),

time: 61.5 us -> 61.4 us (level)
  no operation moved by 1% of the time
where the time goes in v1:
time: 61.4 us; the launch traced here: 61.3 us
  Pallas kernels  59.4 us (97%)
  local copies, waits for them, and re-layouts  1.25 us (2%)
  between operations  0.64 us (1%)
    pallas_call x1, Pallas kernels, body(): pl.pallas_call(kernel, out_shape=(jax.ShapeDtypeStruct((16, 1024), F32),...  59.4 us
    unnamed x2, local copies, waits for them, and re-layouts  1.25 us

profile of v1, /device:TPU:1, one launch (start us, length us, event | category | flops | bytes accessed | tf_op | source)
XLA Modules:
  0.0 61.3 jit_solution(4454235443325684500)
XLA Ops:
  0.6 59.4 %cholesky_step.1 = (f32[16,1024]{1,0:T(8,128)S(1)}, f32[16,512]{1,0:T(8,128)S(1)}) custom-call(f32[1024,256]{1,0:T(8,128)} %a_hbm.1, f32[16,1024]{1,0:T(8,128)} %bitcast.4, f32[16,1024]{1,0:T(8,128)} %bitcast.5, f32[512,512]{1,0:T(8,128)} %inv_hbm.1), custom_call_target="tpu_custom_call" | custom-call | tf_op jit(solution)/shard_map/cholesky_step/pallas_call | solution.py:408
  60.0 0.6 %copy.8 = f32[1024,16]{0,1:T(8,128)} copy(f32[1024,16]{0,1:T(8,128)S(1)} %bitcast.3) | data formatting | bytes 131072
  60.7 0.6 %copy.9 = f32[16,512]{1,0:T(8,128)} copy(f32[16,512]{1,0:T(8,128)S(1)} %get-tuple-element.9) | data formatting | bytes 65536
